TPU v7x, 128 devices: a whole 4x4x4 slice. The times are simulated.
128 devices in a mesh: rep: 8 (over x, z_lo), tm: 4 (over y), space: 4 (over z_hi, core).
Axes of the slice: x: 4, y: 4, z: 4 (z_hi: 2, z_lo: 2; z = z_hi * 2 + z_lo), core: 2. Of those that a mesh axis runs over, the one named last changes fastest.
Arguments:
- query_spatial: bfloat16 [64, 384, 3072], P(('rep', 'tm'), 'space'), parts along dimension 0, may hold values from -16 to 16
- key_spatial: bfloat16 [64, 384, 3072], P(('rep', 'tm'), 'space'), parts along dimension 0, may hold values from -16 to 16
- value_spatial: bfloat16 [64, 384, 3072], P(('rep', 'tm'), 'space'), parts along dimension 0, may hold values from -6 to 6
- query_temporal: bfloat16 [64, 384, 3072], P(('rep', 'tm'), 'space'), parts along dimension 0, may hold values from -16 to 16
- key_temporal: bfloat16 [64, 384, 3072], P(('rep', 'tm'), 'space'), parts along dimension 0, may hold values from -16 to 16
- value_temporal: bfloat16 [64, 384, 3072], P(('rep', 'tm'), 'space'), parts along dimension 0, may hold values from -6 to 6
- upstream: bfloat16 [64, 384, 3072], P(('rep', 'tm'), 'space'), parts along dimension 0, may hold values from -36 to 36
- weight_spatial: bfloat16 [3072, 3072], P('space'), may hold values from -0.109375 to 0.109375
- weight_temporal: bfloat16 [3072, 3072], P('tm'), may hold values from -0.109375 to 0.109375
Outputs:
- grad_query_spatial: bfloat16 [64, 384, 3072], P(('rep', 'tm'), 'space'), parts along dimension 0
- grad_key_spatial: bfloat16 [64, 384, 3072], P(('rep', 'tm'), 'space'), parts along dimension 0
- grad_value_spatial: bfloat16 [64, 384, 3072], P(('rep', 'tm'), 'space'), parts along dimension 0
- grad_query_temporal: bfloat16 [64, 384, 3072], P(('rep', 'tm'), 'space'), parts along dimension 0
- grad_key_temporal: bfloat16 [64, 384, 3072], P(('rep', 'tm'), 'space'), parts along dimension 0
- grad_value_temporal: bfloat16 [64, 384, 3072], P(('rep', 'tm'), 'space'), parts along dimension 0
There are 8 independent parts, one for each index of `rep`. A program takes and returns all parts, laid end to end along the dimension named above; an argument that names none is the same for every part. Nothing has to cross between parts.
All inputs are finite; a program needn't handle non-finite values.
Results may differ from a plain program's by a relative error of at most 0.0076.
Values may be sent and summed in bfloat16 or wider, within the bound.
A program may use at most 192 MiB of HBM per device.

v0:
```python
import jax
import jax.numpy as jnp
from jax import lax
from jax.sharding import PartitionSpec as P

HEAD_DIM = 128


def attention_core(queries, key_rows, value_rows, out_grad, layout):
    key_layout = layout.replace("n", "m")
    scale = HEAD_DIM ** (-0.5)
    to_scores = layout + "," + key_layout + "->bhnm"
    scores = jnp.einsum(to_scores, queries, key_rows, preferred_element_type=jnp.float32) * scale
    attend = jax.nn.softmax(scores, axis=-1)
    attend_low = attend.astype(jnp.bfloat16)
    grad_values = jnp.einsum(
        "bhnm," + layout + "->" + key_layout,
        attend_low,
        out_grad,
        preferred_element_type=jnp.float32,
    )
    grad_attend = jnp.einsum(to_scores, out_grad, value_rows, preferred_element_type=jnp.float32)
    grad_scores = attend * (grad_attend - jnp.sum(attend * grad_attend, axis=-1, keepdims=True))
    scaled_low = (grad_scores * scale).astype(jnp.bfloat16)
    grad_queries = jnp.einsum(
        "bhnm," + key_layout + "->" + layout,
        scaled_low,
        key_rows,
        preferred_element_type=jnp.float32,
    )
    grad_keys = jnp.einsum(
        "bhnm," + layout + "->" + key_layout,
        scaled_low,
        queries,
        preferred_element_type=jnp.float32,
    )
    return (grad_queries.astype(jnp.bfloat16), grad_keys, grad_values)


def split_heads(array):
    return array.reshape(array.shape[0], array.shape[1], array.shape[2] // HEAD_DIM, HEAD_DIM)


def join_heads(array):
    return array.reshape(array.shape[0], array.shape[1], array.shape[2] * array.shape[3])


def spatial_block(query_spatial, key_spatial, value_spatial, upstream, weight_spatial):
    out_grad = jnp.einsum(
        "fsd,id->fsi",
        lax.all_gather(upstream, "space", axis=1, tiled=True),
        weight_spatial,
        preferred_element_type=jnp.float32,
    ).astype(jnp.bfloat16)
    queries, key_rows, value_rows = (
        lax.all_to_all(query_spatial, "space", split_axis=2, concat_axis=1, tiled=True),
        lax.all_to_all(key_spatial, "space", split_axis=2, concat_axis=1, tiled=True),
        lax.all_to_all(value_spatial, "space", split_axis=2, concat_axis=1, tiled=True),
    )
    grads = attention_core(
        split_heads(queries),
        split_heads(key_rows),
        split_heads(value_rows),
        split_heads(out_grad),
        "bnhe",
    )
    return (
        lax.all_to_all(join_heads(grads[0]), "space", split_axis=1, concat_axis=2, tiled=True),
        lax.all_to_all(
            join_heads(grads[1].astype(jnp.bfloat16)),
            "space",
            split_axis=1,
            concat_axis=2,
            tiled=True,
        ),
        lax.all_to_all(
            join_heads(grads[2].astype(jnp.bfloat16)),
            "space",
            split_axis=1,
            concat_axis=2,
            tiled=True,
        ),
    )


def temporal_block(query_temporal, key_temporal, value_temporal, upstream, weight_temporal):
    out_grad = jnp.einsum(
        "fsd,id->fsi",
        lax.all_gather(upstream, "tm", axis=0, tiled=True),
        weight_temporal,
        preferred_element_type=jnp.float32,
    ).astype(jnp.bfloat16)
    queries, key_rows, value_rows = (
        lax.all_to_all(query_temporal, "tm", split_axis=2, concat_axis=0, tiled=True),
        lax.all_to_all(key_temporal, "tm", split_axis=2, concat_axis=0, tiled=True),
        lax.all_to_all(value_temporal, "tm", split_axis=2, concat_axis=0, tiled=True),
    )
    grads = attention_core(
        split_heads(queries),
        split_heads(key_rows),
        split_heads(value_rows),
        split_heads(out_grad),
        "nbhe",
    )
    return (
        lax.all_to_all(join_heads(grads[0]), "tm", split_axis=0, concat_axis=2, tiled=True),
        lax.all_to_all(
            join_heads(grads[1].astype(jnp.bfloat16)), "tm", split_axis=0, concat_axis=2, tiled=True
        ),
        lax.all_to_all(
            join_heads(grads[2].astype(jnp.bfloat16)), "tm", split_axis=0, concat_axis=2, tiled=True
        ),
    )


def local(
    query_spatial,
    key_spatial,
    value_spatial,
    query_temporal,
    key_temporal,
    value_temporal,
    upstream,
    weight_spatial,
    weight_temporal,
):
    spatial = spatial_block(query_spatial, key_spatial, value_spatial, upstream, weight_spatial)
    temporal = temporal_block(
        query_temporal, key_temporal, value_temporal, upstream, weight_temporal
    )
    return (spatial[0], spatial[1], spatial[2], temporal[0], temporal[1], temporal[2])


def solution(mesh):
    in_specs = (
        P(("rep", "tm"), "space", None),
        P(("rep", "tm"), "space", None),
        P(("rep", "tm"), "space", None),
        P(("rep", "tm"), "space", None),
        P(("rep", "tm"), "space", None),
        P(("rep", "tm"), "space", None),
        P(("rep", "tm"), "space", None),
        P("space", None),
        P("tm", None),
    )
    out_specs = (
        P(("rep", "tm"), "space", None),
        P(("rep", "tm"), "space", None),
        P(("rep", "tm"), "space", None),
        P(("rep", "tm"), "space", None),
        P(("rep", "tm"), "space", None),
        P(("rep", "tm"), "space", None),
    )
    return jax.shard_map(local, mesh=mesh, in_specs=in_specs, out_specs=out_specs, check_vma=False)
```

profile of v0, /device:TPU:1, one launch (start us, length us, event | category | flops | bytes accessed | tf_op | source)
XLA Modules:
  0.0 402.6 jit_solution(2487616421696635062)
XLA Ops:
  8.4 3.0 copy.96
  11.4 6.8 %all-to-all-start.1 = ((bf16[2,96,3072]{1,0,2:T(2,128)(2,1)}), bf16[2,96,3072]{1,0,2:T(2,128)(2,1)S(1)}, u32[]{:S(2)}, u32[]{:S(2)}) async-start(bf16[2,96,3072]{1,0,2:T(2,128)(2,1)} %copy.96), calls=%async_computation.1 | async-start | bytes 3145728 | tf_op jit(solution)/shard_map/all_to_all | solution.py:57
  18.2 3.0 copy.101
  21.2 28.7 %all-to-all-done.1 = bf16[2,96,3072]{1,0,2:T(2,128)(2,1)S(1)} async-done(((bf16[2,96,3072]{1,0,2:T(2,128)(2,1)}), bf16[2,96,3072]{1,0,2:T(2,128)(2,1)S(1)}, u32[]{:S(2)}, u32[]{:S(2)}) %all-to-all-start.1) | async-done | bytes 1179680 | tf_op jit(solution)/shard_map/all_to_all | solution.py:57
  49.9 5.2 %all-to-all-start.2 = ((bf16[2,96,3072]{1,0,2:T(2,128)(2,1)}), bf16[2,96,3072]{1,0,2:T(2,128)(2,1)S(1)}, u32[]{:S(2)}, u32[]{:S(2)}) async-start(bf16[2,96,3072]{1,0,2:T(2,128)(2,1)} %copy.101), calls=%async_computation.2 | async-start | bytes 3145728 | tf_op jit(solution)/shard_map/all_to_all | solution.py:58
  55.1 4.4 %copy.94 = bf16[2,96,3072]{1,0,2:T(2,128)(2,1)} copy(bf16[2,96,3072]{2,1,0:T(8,128)(2,1)} %param.9) | data formatting | bytes 2359296 | tf_op args[0]
  59.6 21.8 %all-to-all-done.2 = bf16[2,96,3072]{1,0,2:T(2,128)(2,1)S(1)} async-done(((bf16[2,96,3072]{1,0,2:T(2,128)(2,1)}), bf16[2,96,3072]{1,0,2:T(2,128)(2,1)S(1)}, u32[]{:S(2)}, u32[]{:S(2)}) %all-to-all-start.2) | async-done | bytes 1179680 | tf_op jit(solution)/shard_map/all_to_all | solution.py:58
  81.4 4.9 %all-to-all-start = ((bf16[2,96,3072]{1,0,2:T(2,128)(2,1)}), bf16[2,96,3072]{1,0,2:T(2,128)(2,1)}, u32[]{:S(2)}, u32[]{:S(2)}) async-start(bf16[2,96,3072]{1,0,2:T(2,128)(2,1)} %copy.94), calls=%async_computation | async-start | bytes 3145728 | tf_op jit(solution)/shard_map/all_to_all | solution.py:56
  87.0 4.5 %copy.125 = bf16[2,96,3072]{1,0,2:T(2,128)(2,1)} copy(bf16[2,96,3072]{2,1,0:T(8,128)(2,1)} %param.14) | data formatting | bytes 2359296 | tf_op args[5]
  91.4 15.6 %all-to-all-done = bf16[2,96,3072]{1,0,2:T(2,128)(2,1)} async-done(((bf16[2,96,3072]{1,0,2:T(2,128)(2,1)}), bf16[2,96,3072]{1,0,2:T(2,128)(2,1)}, u32[]{:S(2)}, u32[]{:S(2)}) %all-to-all-start) | async-done | bytes 1179680 | tf_op jit(solution)/shard_map/all_to_all | solution.py:56
  107.1 4.4 %all-to-all-start.8 = ((bf16[2,96,3072]{1,0,2:T(2,128)(2,1)}), bf16[2,96,3072]{1,0,2:T(2,128)(2,1)}, u32[]{:S(2)}, u32[]{:S(2)}) async-start(bf16[2,96,3072]{1,0,2:T(2,128)(2,1)} %copy.125), calls=%async_computation.8 | async-start | bytes 3145728 | tf_op jit(solution)/shard_map/all_to_all | solution.py:96
  111.4 4.5 %copy.121 = bf16[2,96,3072]{1,0,2:T(2,128)(2,1)} copy(bf16[2,96,3072]{2,1,0:T(8,128)(2,1)} %param.13) | data formatting | bytes 2359296 | tf_op args[4]
  115.9 33.2 %all-to-all-done.8 = bf16[2,96,3072]{1,0,2:T(2,128)(2,1)} async-done(((bf16[2,96,3072]{1,0,2:T(2,128)(2,1)}), bf16[2,96,3072]{1,0,2:T(2,128)(2,1)}, u32[]{:S(2)}, u32[]{:S(2)}) %all-to-all-start.8) | async-done | bytes 1179680 | tf_op jit(solution)/shard_map/all_to_all | solution.py:96
  149.1 4.3 %all-to-all-start.7 = ((bf16[2,96,3072]{1,0,2:T(2,128)(2,1)}), bf16[2,96,3072]{1,0,2:T(2,128)(2,1)}, u32[]{:S(2)}, u32[]{:S(2)}) async-start(bf16[2,96,3072]{1,0,2:T(2,128)(2,1)} %copy.121), calls=%async_computation.7 | async-start | bytes 3145728 | tf_op jit(solution)/shard_map/all_to_all | solution.py:95
  153.4 4.5 %copy.119 = bf16[2,96,3072]{1,0,2:T(2,128)(2,1)} copy(bf16[2,96,3072]{2,1,0:T(8,128)(2,1)} %param.12) | data formatting | bytes 2359296 | tf_op args[3]
  157.9 18.1 %all-to-all-done.7 = bf16[2,96,3072]{1,0,2:T(2,128)(2,1)} async-done(((bf16[2,96,3072]{1,0,2:T(2,128)(2,1)}), bf16[2,96,3072]{1,0,2:T(2,128)(2,1)}, u32[]{:S(2)}, u32[]{:S(2)}) %all-to-all-start.7) | async-done | bytes 1179680 | tf_op jit(solution)/shard_map/all_to_all | solution.py:95
  175.9 4.7 %all-to-all-start.6 = ((bf16[2,96,3072]{1,0,2:T(2,128)(2,1)}), bf16[2,96,3072]{1,0,2:T(2,128)(2,1)}, u32[]{:S(2)}, u32[]{:S(2)}) async-start(bf16[2,96,3072]{1,0,2:T(2,128)(2,1)} %copy.119), calls=%async_computation.6 | async-start | bytes 3145728 | tf_op jit(solution)/shard_map/all_to_all | solution.py:94
  183.4 2.8 reshape.67
  190.4 4.8 %copy.95 = bf16[2,96,4,768]{3,1,2,0:T(8,128)(2,1)} copy(bf16[2,96,4,768]{1,0,3,2:T(2,128)(2,1)} %bitcast) | data formatting | bytes 2359296 | tf_op jit(solution)/shard_map/all_to_all | solution.py:56
  195.2 2.8 reshape.66
  199.7 3.5 copy.126
  205.5 3.5 copy.122
  211.2 4.7 %copy.120 = bf16[2,96,4,768]{3,1,0,2:T(8,128)(2,1)} copy(bf16[2,96,4,768]{1,0,3,2:T(2,128)(2,1)} %bitcast.20) | data formatting | bytes 2359296 | tf_op jit(solution)/shard_map/all_to_all | solution.py:94
  218.8 7.3 %fusion.78 = (f32[2,6,384]{2,1,0:T(8,128)S(1)}, f32[2,6,384,384]{2,3,1,0:T(8,128)}) fusion(bf16[2,384,6,128]{1,3,2,0:T(8,128)(2,1)} %copy.111, bf16[2,384,6,128]{1,3,2,0:T(8,128)(2,1)} %copy.106), kind=kOutput, calls=%fused_computation.64 | convolution fusion | flops 458293632 | bytes 9455616 | tf_op jit(solution)/shard_map/sub | solution.py:14
  226.1 8.7 %fusion.42 = bf16[2,384,768]{2,1,0:T(8,128)(2,1)} fusion(bf16[2,384,3072]{2,1,0:T(8,128)(2,1)} %all-gather.3.cloned.1.call-done, bf16[768,3072]{1,0:T(8,128)(2,1)} %param.16), kind=kOutput, calls=%fused_computation.32 | convolution fusion | flops 3624468480 | bytes 10616832 | tf_op jit(solution)/shard_map/fsd,id->fsi/dot_general | solution.py:49
  234.8 2.9 copy.100
  237.7 5.3 %fusion.53 = f32[2,6,384,384]{2,3,1,0:T(8,128)} fusion(bf16[2,384,6,128]{1,3,2,0:T(8,128)(2,1)} %bitcast.92, bf16[2,384,6,128]{3,2,1,0:T(8,128)(2,1)S(1)} %reshape.69), kind=kOutput, calls=%fused_computation.42 | convolution fusion | flops 452984832 | bytes 9437184 | tf_op jit(solution)/shard_map/bnhe,bmhe->bhnm/dot_general | solution.py:22
  243.0 11.6 %fusion.36 = bf16[2,6,384,128]{2,3,1,0:T(8,128)(2,1)S(1)} fusion(bf16[2,384,6,128]{1,3,2,0:T(8,128)(2,1)} %copy.106, f32[2,6,384,384]{2,3,1,0:T(8,128)} %fusion.53, f32[2,6,384,384]{2,3,1,0:T(8,128)} %get-tuple-element.7, f32[2,6,384]{2,1,0:T(8,128)S(1)} %get-tuple-element.6), kind=kOutput, calls=%fused_computation.30 | convolution fusion | flops 465965952 | bytes 16533504 | tf_op jit(solution)/shard_map/bhnm,bmhe->bnhe/dot_general | solution.py:25
  254.6 2.8 copy.107
  257.4 5.7 %all-to-all-start.3 = ((bf16[2,384,768]{2,0,1:T(2,128)(2,1)}), bf16[2,384,768]{2,0,1:T(2,128)(2,1)}, u32[]{:S(2)}, u32[]{:S(2)}) async-start(bf16[2,384,768]{2,0,1:T(2,128)(2,1)} %copy.107), calls=%async_computation.3 | async-start | bytes 2359296 | tf_op jit(solution)/shard_map/all_to_all | solution.py:68
  267.1 11.7 %fusion.39 = bf16[2,6,384,128]{2,3,1,0:T(8,128)(2,1)S(1)} fusion(bf16[2,384,6,128]{1,3,2,0:T(8,128)(2,1)} %copy.111, f32[2,6,384,384]{2,3,1,0:T(8,128)} %fusion.53, f32[2,6,384,384]{2,3,1,0:T(8,128)} %get-tuple-element.7, f32[2,6,384]{2,1,0:T(8,128)S(1)} %copy-done.9), kind=kOutput, calls=%fused_computation.31 | convolution fusion | flops 465965952 | bytes 16533504 | tf_op jit(solution)/shard_map/bhnm,bnhe->bmhe/dot_general | solution.py:31
  278.8 2.8 copy.112
  281.6 4.9 %all-to-all-start.4 = ((bf16[2,384,768]{2,0,1:T(2,128)(2,1)}), bf16[2,384,768]{2,0,1:T(2,128)(2,1)}, u32[]{:S(2)}, u32[]{:S(2)}) async-start(bf16[2,384,768]{2,0,1:T(2,128)(2,1)} %copy.112), calls=%async_computation.4 | async-start | bytes 2359296 | tf_op jit(solution)/shard_map/all_to_all | solution.py:69
  286.6 5.2 %fusion.33 = bf16[2,6,128,384]{3,2,1,0:T(8,128)(2,1)} fusion(bf16[2,384,6,128]{1,3,2,0:T(8,128)(2,1)S(1)} %bitcast.93, f32[2,6,384,384]{2,3,1,0:T(8,128)} %get-tuple-element.7, f32[2,6,384]{2,1,0:T(8,128)S(1)} %copy-done.9), kind=kOutput, calls=%fused_computation.29 | convolution fusion | flops 457113600 | bytes 9455616 | tf_op jit(solution)/shard_map/bhnm,bnhe->bmhe/dot_general | solution.py:16
  291.8 4.7 %copy.116 = bf16[2,384,768]{2,0,1:T(2,128)(2,1)} copy(bf16[2,384,768]{1,2,0:T(8,128)(2,1)} %bitcast.111) | data formatting | bytes 2359296 | tf_op jit(solution)/shard_map/reshape | solution.py:45
  296.5 6.6 %all-to-all-done.4 = bf16[2,384,768]{2,0,1:T(2,128)(2,1)} async-done(((bf16[2,384,768]{2,0,1:T(2,128)(2,1)}), bf16[2,384,768]{2,0,1:T(2,128)(2,1)}, u32[]{:S(2)}, u32[]{:S(2)}) %all-to-all-start.4) | async-done | bytes 1179680 | tf_op jit(solution)/shard_map/all_to_all | solution.py:69
  303.2 5.3 %all-to-all-start.5 = ((bf16[2,384,768]{2,0,1:T(2,128)(2,1)}), bf16[2,384,768]{2,0,1:T(2,128)(2,1)}, u32[]{:S(2)}, u32[]{:S(2)}) async-start(bf16[2,384,768]{2,0,1:T(2,128)(2,1)} %copy.116), calls=%async_computation.5 | async-start | bytes 2359296 | tf_op jit(solution)/shard_map/all_to_all | solution.py:76
  308.5 8.6 %fusion.45 = bf16[8,96,768]{2,1,0:T(8,128)(2,1)} fusion(bf16[8,96,3072]{2,1,0:T(8,128)(2,1)} %all-gather.5.cloned.1.call-done, bf16[768,3072]{1,0:T(8,128)(2,1)} %param.17), kind=kOutput, calls=%fused_computation.33 | convolution fusion | flops 3624468480 | bytes 10616832 | tf_op jit(solution)/shard_map/fsd,id->fsi/dot_general | solution.py:87
  317.1 3.9 reshape.75
  321.0 4.3 %fusion.51 = f32[96,6,8,8]{2,3,1,0:T(8,128)} fusion(bf16[8,96,6,128]{3,2,1,0:T(8,128)(2,1)S(1)} %copy-done.2, bf16[8,96,6,128]{3,2,1,0:T(8,128)(2,1)} %reshape.75), kind=kOutput, calls=%fused_computation.40 | convolution fusion | flops 9437184 | bytes 2506752 | tf_op jit(solution)/shard_map/nbhe,mbhe->bhnm/dot_general | solution.py:22
  325.3 6.4 %fusion.48 = bf16[8,96,6,128]{3,0,2,1:T(8,128)(2,1)} fusion(f32[96,6,8,8]{2,3,1,0:T(8,128)} %fusion.51, bf16[8,96,6,128]{3,2,1,0:T(8,128)(2,1)S(1)} %copy-done.3, f32[96,6,8,8]{2,3,1,0:T(8,128)} %get-tuple-element.9, f32[96,6,8]{2,1,0:T(8,128)S(1)} %get-tuple-element.8), kind=kOutput, calls=%fused_computation.37 | convolution fusion | flops 10289671 | bytes 2672640 | tf_op jit(solution)/shard_map/bhnm,mbhe->nbhe/dot_general | solution.py:25
  335.5 4.6 %all-to-all-start.9 = ((bf16[8,96,768]{2,1,0:T(8,128)(2,1)}), bf16[8,96,768]{2,1,0:T(8,128)(2,1)S(1)}, u32[]{:S(2)}, u32[]{:S(2)}) async-start(bf16[8,96,768]{2,1,0:T(8,128)(2,1)} %reshape.77), calls=%async_computation.9 | async-start | bytes 2359296 | tf_op jit(solution)/shard_map/all_to_all | solution.py:106
  340.2 6.5 %fusion.49 = bf16[8,96,6,128]{3,0,2,1:T(8,128)(2,1)} fusion(f32[96,6,8,8]{2,3,1,0:T(8,128)} %fusion.51, bf16[8,96,6,128]{3,2,1,0:T(8,128)(2,1)S(1)} %copy-done.1, f32[96,6,8,8]{2,3,1,0:T(8,128)} %get-tuple-element.9, f32[96,6,8]{2,1,0:T(8,128)S(1)} %get-tuple-element.8), kind=kOutput, calls=%fused_computation.38 | convolution fusion | flops 10289671 | bytes 2672640 | tf_op jit(solution)/shard_map/bhnm,nbhe->mbhe/dot_general | solution.py:31
  350.4 6.1 %all-to-all-done.9 = bf16[8,96,768]{2,1,0:T(8,128)(2,1)S(1)} async-done(((bf16[8,96,768]{2,1,0:T(8,128)(2,1)}), bf16[8,96,768]{2,1,0:T(8,128)(2,1)S(1)}, u32[]{:S(2)}, u32[]{:S(2)}) %all-to-all-start.9) | async-done | bytes 1179680 | tf_op jit(solution)/shard_map/all_to_all | solution.py:106
  356.5 4.5 %all-to-all-start.10 = ((bf16[8,96,768]{2,1,0:T(8,128)(2,1)}), bf16[8,96,768]{2,1,0:T(8,128)(2,1)}, u32[]{:S(2)}, u32[]{:S(2)}) async-start(bf16[8,96,768]{2,1,0:T(8,128)(2,1)} %reshape.78), calls=%async_computation.10 | async-start | bytes 2359296 | tf_op jit(solution)/shard_map/all_to_all | solution.py:107
  366.2 10.2 %all-to-all-done.10 = bf16[8,96,768]{2,1,0:T(8,128)(2,1)} async-done(((bf16[8,96,768]{2,1,0:T(8,128)(2,1)}), bf16[8,96,768]{2,1,0:T(8,128)(2,1)}, u32[]{:S(2)}, u32[]{:S(2)}) %all-to-all-start.10) | async-done | bytes 1179680 | tf_op jit(solution)/shard_map/all_to_all | solution.py:107
  376.4 3.5 all-to-all-start.11
  391.2 3.2 all-to-all-done.11
  (55 shorter events, 47.1 us)
Async XLA Ops:
  7.2 1.3 copy-start.6
  7.2 219.0 %all-gather.3.cloned.1.call-start = ((), (), s32[]{:S(2)}) async-start(), calls=%async_computation.12 | async-start | bytes 5898240 | tf_op jit(solution)/shard_map/all_gather | solution.py:51
  11.4 6.8 %copy-start.7 = (bf16[2,96,3072]{2,1,0:T(8,128)(2,1)S(1)}, bf16[2,96,3072]{2,1,0:T(8,128)(2,1)}, u32[]{:S(2)}) copy-start(bf16[2,96,3072]{2,1,0:T(8,128)(2,1)} %param.11) | copy-start | bytes 3538948
  11.4 38.5 %all-to-all-start.1 = ((bf16[2,96,3072]{1,0,2:T(2,128)(2,1)}), bf16[2,96,3072]{1,0,2:T(2,128)(2,1)S(1)}, u32[]{:S(2)}, u32[]{:S(2)}) async-start(bf16[2,96,3072]{1,0,2:T(2,128)(2,1)} %copy.96), calls=%async_computation.1 | async-start | bytes 3145728 | tf_op jit(solution)/shard_map/all_to_all | solution.py:57
  49.9 31.5 %all-to-all-start.2 = ((bf16[2,96,3072]{1,0,2:T(2,128)(2,1)}), bf16[2,96,3072]{1,0,2:T(2,128)(2,1)S(1)}, u32[]{:S(2)}, u32[]{:S(2)}) async-start(bf16[2,96,3072]{1,0,2:T(2,128)(2,1)} %copy.101), calls=%async_computation.2 | async-start | bytes 3145728 | tf_op jit(solution)/shard_map/all_to_all | solution.py:58
  81.4 25.7 %all-to-all-start = ((bf16[2,96,3072]{1,0,2:T(2,128)(2,1)}), bf16[2,96,3072]{1,0,2:T(2,128)(2,1)}, u32[]{:S(2)}, u32[]{:S(2)}) async-start(bf16[2,96,3072]{1,0,2:T(2,128)(2,1)} %copy.94), calls=%async_computation | async-start | bytes 3145728 | tf_op jit(solution)/shard_map/all_to_all | solution.py:56
  86.2 222.2 %all-gather.5.cloned.1.call-start = ((), (), s32[]{:S(2)}) async-start(), calls=%async_computation.13 | async-start | bytes 5898240 | tf_op jit(solution)/shard_map/all_gather | solution.py:89
  107.1 42.0 %all-to-all-start.8 = ((bf16[2,96,3072]{1,0,2:T(2,128)(2,1)}), bf16[2,96,3072]{1,0,2:T(2,128)(2,1)}, u32[]{:S(2)}, u32[]{:S(2)}) async-start(bf16[2,96,3072]{1,0,2:T(2,128)(2,1)} %copy.125), calls=%async_computation.8 | async-start | bytes 3145728 | tf_op jit(solution)/shard_map/all_to_all | solution.py:96
  149.1 26.9 %all-to-all-start.7 = ((bf16[2,96,3072]{1,0,2:T(2,128)(2,1)}), bf16[2,96,3072]{1,0,2:T(2,128)(2,1)}, u32[]{:S(2)}, u32[]{:S(2)}) async-start(bf16[2,96,3072]{1,0,2:T(2,128)(2,1)} %copy.121), calls=%async_computation.7 | async-start | bytes 3145728 | tf_op jit(solution)/shard_map/all_to_all | solution.py:95
  175.9 35.3 %all-to-all-start.6 = ((bf16[2,96,3072]{1,0,2:T(2,128)(2,1)}), bf16[2,96,3072]{1,0,2:T(2,128)(2,1)}, u32[]{:S(2)}, u32[]{:S(2)}) async-start(bf16[2,96,3072]{1,0,2:T(2,128)(2,1)} %copy.119), calls=%async_computation.6 | async-start | bytes 3145728 | tf_op jit(solution)/shard_map/all_to_all | solution.py:94
  218.8 44.3 %copy-start = (bf16[8,96,6,128]{3,2,1,0:T(8,128)(2,1)}, bf16[8,96,6,128]{3,2,1,0:T(8,128)(2,1)S(1)}, u32[]{:S(2)}) copy-start(bf16[8,96,6,128]{3,2,1,0:T(8,128)(2,1)S(1)} %reshape.73) | copy-start | bytes 3538948
  226.1 16.8 %copy-start.8 = (f32[2,6,384]{2,1,0:T(8,128)}, f32[2,6,384]{2,1,0:T(8,128)S(1)}, u32[]{:S(2)}) copy-start(f32[2,6,384]{2,1,0:T(8,128)S(1)} %get-tuple-element.6) | copy-start | bytes 55300
  257.4 5.7 %copy-start.3 = (bf16[8,96,6,128]{3,2,1,0:T(8,128)(2,1)S(1)}, bf16[8,96,6,128]{3,2,1,0:T(8,128)(2,1)}, u32[]{:S(2)}) copy-start(bf16[8,96,6,128]{3,2,1,0:T(8,128)(2,1)} %reshape.74) | copy-start | bytes 3538948
  257.4 24.2 %all-to-all-start.3 = ((bf16[2,384,768]{2,0,1:T(2,128)(2,1)}), bf16[2,384,768]{2,0,1:T(2,128)(2,1)}, u32[]{:S(2)}, u32[]{:S(2)}) async-start(bf16[2,384,768]{2,0,1:T(2,128)(2,1)} %copy.107), calls=%async_computation.3 | async-start | bytes 2359296 | tf_op jit(solution)/shard_map/all_to_all | solution.py:68
  264.6 2.5 copy-start.9
  281.6 4.9 %copy-start.5 = (bf16[2,384,768]{1,2,0:T(8,128)(2,1)S(1)}, bf16[2,384,768]{1,2,0:T(8,128)(2,1)}, u32[]{:S(2)}) copy-start(bf16[2,384,768]{1,2,0:T(8,128)(2,1)} %copy.100) | copy-start | bytes 3538948
  281.6 21.5 %all-to-all-start.4 = ((bf16[2,384,768]{2,0,1:T(2,128)(2,1)}), bf16[2,384,768]{2,0,1:T(2,128)(2,1)}, u32[]{:S(2)}, u32[]{:S(2)}) async-start(bf16[2,384,768]{2,0,1:T(2,128)(2,1)} %copy.112), calls=%async_computation.4 | async-start | bytes 2359296 | tf_op jit(solution)/shard_map/all_to_all | solution.py:69
  303.2 32.4 %all-to-all-start.5 = ((bf16[2,384,768]{2,0,1:T(2,128)(2,1)}), bf16[2,384,768]{2,0,1:T(2,128)(2,1)}, u32[]{:S(2)}, u32[]{:S(2)}) async-start(bf16[2,384,768]{2,0,1:T(2,128)(2,1)} %copy.116), calls=%async_computation.5 | async-start | bytes 2359296 | tf_op jit(solution)/shard_map/all_to_all | solution.py:76
  317.1 3.9 copy-start.2
  335.5 4.6 %copy-start.1 = (bf16[8,96,6,128]{3,2,1,0:T(8,128)(2,1)S(1)}, bf16[8,96,6,128]{3,2,1,0:T(8,128)(2,1)}, u32[]{:S(2)}) copy-start(bf16[8,96,6,128]{3,2,1,0:T(8,128)(2,1)} %copy-done) | copy-start | bytes 3538948
  335.5 20.9 %all-to-all-start.9 = ((bf16[8,96,768]{2,1,0:T(8,128)(2,1)}), bf16[8,96,768]{2,1,0:T(8,128)(2,1)S(1)}, u32[]{:S(2)}, u32[]{:S(2)}) async-start(bf16[8,96,768]{2,1,0:T(8,128)(2,1)} %reshape.77), calls=%async_computation.9 | async-start | bytes 2359296 | tf_op jit(solution)/shard_map/all_to_all | solution.py:106
  350.4 10.6 %copy-start.4 = (bf16[8,96,6,128]{3,2,1,0:T(8,128)(2,1)S(1)}, bf16[8,96,6,128]{3,2,1,0:T(8,128)(2,1)}, u32[]{:S(2)}) copy-start(bf16[8,96,6,128]{3,2,1,0:T(8,128)(2,1)} %reshape.75) | copy-start | bytes 3538948
  356.5 19.9 %all-to-all-start.10 = ((bf16[8,96,768]{2,1,0:T(8,128)(2,1)}), bf16[8,96,768]{2,1,0:T(8,128)(2,1)}, u32[]{:S(2)}, u32[]{:S(2)}) async-start(bf16[8,96,768]{2,1,0:T(8,128)(2,1)} %reshape.78), calls=%async_computation.10 | async-start | bytes 2359296 | tf_op jit(solution)/shard_map/all_to_all | solution.py:107
  376.4 18.0 %all-to-all-start.11 = ((bf16[8,96,768]{2,1,0:T(8,128)(2,1)}), bf16[8,96,768]{2,1,0:T(8,128)(2,1)S(1)}, u32[]{:S(2)}, u32[]{:S(2)}) async-start(bf16[8,96,768]{2,1,0:T(8,128)(2,1)} %reshape.79), calls=%async_computation.11 | async-start | bytes 2359296 | tf_op jit(solution)/shard_map/all_to_all | solution.py:110
Sparse Core Ops, SparseCore 0:
  9.7 61.7 all-gather.2
  88.7 71.9 all-gather.4
where the time goes:
time: 409 us; the launch traced here: 403 us
  waiting for transfers between devices  145 us (35%)
  local copies, waits for them, and re-layouts  102 us (25%)
  matrix products  79.7 us (19%)
  starting transfers between devices  58.9 us (14%)
  between operations  14.5 us (4%)
    all_to_all x1, waiting for transfers between devices, temporal_block(): lax.all_to_all(value_temporal, 'tm', split_axis=2, concat_axis=0, tiled=T...  33.2 us
    all_to_all x1, waiting for transfers between devices, spatial_block(): lax.all_to_all(key_spatial, 'space', split_axis=2, concat_axis=1, tiled=T...  28.7 us
    unnamed x26, local copies, waits for them, and re-layouts  24.3 us
    all_to_all x1, waiting for transfers between devices, spatial_block(): lax.all_to_all(value_spatial, 'space', split_axis=2, concat_axis=1, tiled...  21.8 us
    reshape x9, local copies, waits for them, and re-layouts, split_heads(): array.reshape(array.shape[0], array.shape[1], array.shape[2] // HEAD_DIM,...  21.6 us
    dot_general x2, matrix products, attention_core(): jnp.einsum('bhnm,' + layout + '->' + key_layout, scaled_low, queries, pre...  18.1 us
    all_to_all x1, waiting for transfers between devices, temporal_block(): lax.all_to_all(key_temporal, 'tm', split_axis=2, concat_axis=0, tiled=True)  18.1 us
    dot_general x2, matrix products, attention_core(): jnp.einsum('bhnm,' + key_layout + '->' + layout, scaled_low, key_rows, pr...  18 us
  transfers between devices with their start and end apart: 14, of which 9 were waited for; matrix products, arithmetic and copies ran while one was open for 45% of the time, Pallas kernels for 0%

commit v1 on v0

v1 whole, which is shorter than its diff:
```python
import functools

import jax
import jax.numpy as jnp
from jax import lax
from jax.experimental import pallas as pl
from jax.experimental.pallas import tpu as pltpu
from jax.sharding import PartitionSpec as P

HEAD = 128
SCALE = HEAD ** (-0.5)
MESH = pl.DeviceIdType.MESH
STEP = 16
BEFORE_SPATIAL = (2, 4)
NT = (((1,), (1,)), ((), ()))
NN = (((1,), (0,)), ((), ()))
TN = (((0,), (0,)), ((), ()))


def mul(a, b, dims):
    return lax.dot_general(a, b, dims, preferred_element_type=jnp.float32)


def attention(q, k, v, o, mask):
    scores = mul(k, q, NT) * SCALE
    if mask is not None:
        scores = jnp.where(mask, scores, -3.0e38)
    e = jnp.exp(scores - jnp.max(scores, axis=0, keepdims=True))
    a = e * (1.0 / jnp.sum(e, axis=0, keepdims=True))
    gv = mul(a.astype(jnp.bfloat16), o, NN)
    da = mul(v, o, NT)
    ds = a * (da - jnp.sum(a * da, axis=0, keepdims=True))
    low = (ds * SCALE).astype(jnp.bfloat16)
    gk = mul(low, q, NN)
    gq = mul(low, k, TN)
    return gq.astype(jnp.bfloat16), gk.astype(jnp.bfloat16), gv.astype(jnp.bfloat16)


def core(qs, ks, vs, qt, kt, vt, up, ws, wt, out,
         up_s, up_t, a_s, a_t, w_s, w_t, og_s, og_t, g_s, g_t,
         own_sem, upz_sem, qkvz_sem, upy_sem, qkvy_sem, gz_sem, gy_sem, send_sem):
    frames, rows, width = up.shape
    part = a_s.shape[-1]
    heads = part // HEAD
    steps = rows // STEP
    t = lax.axis_index("tm")
    s = lax.axis_index("space")
    n = 4
    y_up, y_down, y_far = lax.rem(t + 1, n), lax.rem(t + n - 1, n), lax.rem(t + 2, n)
    pair = s + 1 - 2 * lax.rem(s, 2)
    far = lax.rem(s + 2, n)
    cross = lax.rem(pair + 2, n)

    barrier = pltpu.get_barrier_semaphore()
    for d in (y_up, y_down, y_far):
        pl.semaphore_signal(barrier, inc=1, device_id={"tm": d}, device_id_type=MESH)
    for d in (pair, far, cross):
        pl.semaphore_signal(barrier, inc=1, device_id={"space": d}, device_id_type=MESH)

    def cols(d):
        return pl.ds(pl.multiple_of(d * part, part), part)

    def tokens(d):
        return pl.ds(pl.multiple_of(d * rows, rows), rows)

    def toks(i):
        return pl.ds(pl.multiple_of(i * STEP, STEP), STEP)

    def remote(src, dst, sem, **where):
        return pltpu.make_async_remote_copy(
            src, dst, send_sem.at[0], sem, device_id=where, device_id_type=MESH)

    def arrived(ref, sem):
        pltpu.make_async_copy(ref, ref, sem).wait()

    own = [
        pltpu.make_async_copy(up, up_t.at[pl.ds(2 * t, 2)], own_sem.at[0]),
        pltpu.make_async_copy(wt, w_t, own_sem.at[1]),
        pltpu.make_async_copy(up, up_s.at[:, tokens(s)], own_sem.at[2]),
        pltpu.make_async_copy(ws, w_s, own_sem.at[3]),
    ]
    for j, (src_t, src_s) in enumerate(((qt, qs), (kt, ks), (vt, vs))):
        own.append(pltpu.make_async_copy(src_t.at[:, :, cols(t)], a_t.at[j, pl.ds(2 * t, 2)], own_sem.at[4 + j]))
        own.append(pltpu.make_async_copy(src_s.at[:, :, cols(s)], a_s.at[j, :, tokens(s)], own_sem.at[7 + j]))
    for copy in own:
        copy.start()
    pl.semaphore_wait(barrier, 6)

    def send_space(f):
        for d, slot in ((far, 0), (pair, 1)):
            remote(up.at[f], up_s.at[f, tokens(s)], upz_sem.at[f, slot], space=d).start()
        for j, src in enumerate((qs, ks, vs)):
            for d in (far, cross, pair):
                remote(src.at[f, :, cols(d)], a_s.at[j, f, tokens(s)], qkvz_sem.at[f], space=d).start()

    def send_time(i):
        for d, slot in ((y_up, 0), (y_down, 1)):
            remote(up.at[:, toks(i)], up_t.at[pl.ds(2 * t, 2), toks(i)], upy_sem.at[i, slot], tm=d).start()
        for j, src in enumerate((qt, kt, vt)):
            for d in (y_up, y_down, y_far):
                remote(src.at[:, toks(i), cols(d)], a_t.at[j, pl.ds(2 * t, 2), toks(i)], qkvy_sem.at[i], tm=d).start()

    def pass_time(i):
        arrived(up_t.at[pl.ds(0, 2), toks(i)], upy_sem.at[i, 0])
        low = 2 * y_down
        remote(up_t.at[low, toks(i)], up_t.at[low, toks(i)], upy_sem.at[i, 2], tm=y_up).start()
        arrived(up_t.at[pl.ds(0, 2), toks(i)], upy_sem.at[i, 1])
        high = 2 * y_up + 1
        remote(up_t.at[high, toks(i)], up_t.at[high, toks(i)], upy_sem.at[i, 3], tm=y_down).start()

    def finish_time(i):
        arrived(up_t.at[0, toks(i)], upy_sem.at[i, 2])
        arrived(up_t.at[0, toks(i)], upy_sem.at[i, 3])
        arrived(a_t.at[:, pl.ds(0, 6), toks(i)], qkvy_sem.at[i])

    def time_step(i):
        x = up_t[:, toks(i), :].reshape(8 * STEP, width)
        og_t[...] = mul(x, w_t[...], NT).astype(jnp.bfloat16)
        size = 8 * STEP
        mask = (lax.broadcasted_iota(jnp.int32, (size, size), 0) % STEP
                == lax.broadcasted_iota(jnp.int32, (size, size), 1) % STEP)
        for h in range(heads):
            c = slice(h * HEAD, (h + 1) * HEAD)
            q, k, v = (a_t[j, :, toks(i), c].reshape(size, HEAD) for j in range(3))
            for j, g in enumerate(attention(q, k, v, og_t[:, c], mask)):
                g_t[j, :, toks(i), c] = g.reshape(8, STEP, HEAD)
        pltpu.make_async_copy(g_t.at[:, pl.ds(2 * t, 2), toks(i)], out.at[pl.ds(3, 3), :, toks(i), cols(t)], gy_sem.at[1]).start()
        for d in (y_far, y_up, y_down):
            remote(g_t.at[:, pl.ds(2 * d, 2), toks(i)], out.at[pl.ds(3, 3), :, toks(i), cols(t)], gy_sem.at[0], tm=d).start()

    def space_part(f):
        arrived(up_s.at[f, pl.ds(0, rows)], upz_sem.at[f, 0])
        remote(up_s.at[f, tokens(far)], up_s.at[f, tokens(far)], upz_sem.at[f, 2], space=pair).start()
        arrived(up_s.at[f, pl.ds(0, rows)], upz_sem.at[f, 1])
        arrived(up_s.at[f, pl.ds(0, rows)], upz_sem.at[f, 2])
        arrived(a_s.at[:, f, pl.ds(0, 3 * rows)], qkvz_sem.at[f])
        og_s[...] = mul(up_s[f], w_s[...], NT).astype(jnp.bfloat16)

        def head(h, carry):
            c = pl.ds(pl.multiple_of(h * HEAD, HEAD), HEAD)
            q, k, v = (a_s[j, f, :, c] for j in range(3))
            for j, g in enumerate(attention(q, k, v, og_s[:, c], None)):
                g_s[j, f, :, c] = g
            return carry

        half = heads // 2
        for b in range(2):
            lax.fori_loop(b * half, (b + 1) * half, head, 0)
            here = pl.ds(b * half * HEAD, half * HEAD)
            there = pl.ds(pl.multiple_of(s * part + b * half * HEAD, HEAD), half * HEAD)
            pltpu.make_async_copy(g_s.at[:, f, tokens(s), here], out.at[pl.ds(0, 3), f, :, there], gz_sem.at[1]).start()
            for d in (far, cross, pair):
                remote(g_s.at[:, f, tokens(d), here], out.at[pl.ds(0, 3), f, :, there], gz_sem.at[0], space=d).start()

    send_space(0)
    for i in range(steps):
        send_time(i)
        if i == 2:
            send_space(1)
    pass_time(0)
    for copy in own:
        copy.wait()

    def step(i, carry):
        @pl.when(i + 1 < steps)
        def _():
            pass_time(i + 1)

        finish_time(i)
        time_step(i)

        @pl.when((i == BEFORE_SPATIAL[0]) | (i == BEFORE_SPATIAL[1]))
        def _():
            space_part(jnp.where(i == BEFORE_SPATIAL[0], 0, 1))
        return carry

    lax.fori_loop(0, steps, step, 0)

    arrived(out.at[pl.ds(0, 3), :, :, pl.ds(0, part)], gz_sem.at[1])
    arrived(out.at[pl.ds(0, 3), :, :, pl.ds(0, 3 * part)], gz_sem.at[0])
    arrived(out.at[pl.ds(3, 3), :, :, pl.ds(0, part)], gy_sem.at[1])
    arrived(out.at[pl.ds(3, 3), :, :, pl.ds(0, 3 * part)], gy_sem.at[0])
    for _ in range(6):
        arrived(up_t.at[pl.ds(0, 2)], send_sem.at[0])
    for ref in (a_s.at[:, :, pl.ds(0, 3 * rows)], a_t.at[:, pl.ds(0, 6)]):
        arrived(ref, send_sem.at[0])
        arrived(ref, send_sem.at[0])


def split(whole, *rest):
    outs, sem = rest[:-1], rest[-1]
    copies = [pltpu.make_async_copy(whole.at[j], o, sem.at[j]) for j, o in enumerate(outs)]
    for copy in copies:
        copy.start()
    for copy in copies:
        copy.wait()


def local(*args):
    up, ws = args[6], args[7]
    frames, rows, width = up.shape
    part = ws.shape[0]
    bf = jnp.bfloat16
    anywhere = pl.BlockSpec(memory_space=pl.ANY)
    whole = pl.pallas_call(
        core,
        out_shape=jax.ShapeDtypeStruct((6, frames, rows, width), bf),
        in_specs=[anywhere] * 9,
        out_specs=anywhere,
        scratch_shapes=[
            pltpu.VMEM((frames, 4 * rows, width), bf),
            pltpu.VMEM((4 * frames, rows, width), bf),
            pltpu.VMEM((3, frames, 4 * rows, part), bf),
            pltpu.VMEM((3, 4 * frames, rows, part), bf),
            pltpu.VMEM((part, width), bf),
            pltpu.VMEM((part, width), bf),
            pltpu.VMEM((4 * rows, part), bf),
            pltpu.VMEM((4 * frames * STEP, part), bf),
            pltpu.VMEM((3, frames, 4 * rows, part), bf),
            pltpu.VMEM((3, 4 * frames, rows, part), bf),
            pltpu.SemaphoreType.DMA((10,)),
            pltpu.SemaphoreType.DMA((frames, 3)),
            pltpu.SemaphoreType.DMA((frames,)),
            pltpu.SemaphoreType.DMA((rows // STEP, 4)),
            pltpu.SemaphoreType.DMA((rows // STEP,)),
            pltpu.SemaphoreType.DMA((2,)),
            pltpu.SemaphoreType.DMA((2,)),
            pltpu.SemaphoreType.DMA((1,)),
        ],
        compiler_params=pltpu.CompilerParams(
            collective_id=0, has_side_effects=True, vmem_limit_bytes=56 * 1024 * 1024),
        name="core",
    )(*args)
    one = jax.ShapeDtypeStruct((frames, rows, width), bf)
    return tuple(pl.pallas_call(
        split,
        out_shape=[one] * 6,
        in_specs=[anywhere],
        out_specs=[anywhere] * 6,
        scratch_shapes=[pltpu.SemaphoreType.DMA((6,))],
        name="split",
    )(whole))


def solution(mesh):
    rows = P(("rep", "tm"), "space", None)
    in_specs = (rows,) * 7 + (P("space", None), P("tm", None))
    return jax.shard_map(local, mesh=mesh, in_specs=in_specs, out_specs=(rows,) * 6, check_vma=False)
```

time: 409 us -> 358 us (0.88); the launches traced: 403 us -> 358 us
  Pallas kernels: 0 us -> 357 us
  waiting for transfers between devices: 145 us -> 0 us
  local copies, waits for them, and re-layouts: 102 us -> 0 us
  matrix products: 79.7 us -> 0 us
  starting transfers between devices: 58.9 us -> 0 us
  between operations: 14.5 us -> 0.64 us
    pallas_call x0 -> x2, Pallas kernels: none -> 357 us  [the longest x1 216 us: local(): pl.pallas_call(split, out_shape=[one] * 6, in_specs=[anywhere], out_specs...]
    all_to_all x12 -> x0, waiting for transfers between devices: 143 us -> none  [the longest x1 33.2 us: temporal_block(): lax.all_to_all(value_temporal, 'tm', split_axis=2, concat_axis=0, tiled=T...]
    dot_general x11 -> x0, matrix products: 72.4 us -> none  [the longest x2 18.1 us: attention_core(): jnp.einsum('bhnm,' + layout + '->' + key_layout, scaled_low, queries, pre...]
    all_to_all x12 -> x0, starting transfers between devices: 58.8 us -> none  [the longest x1 6.78 us: spatial_block(): lax.all_to_all(key_spatial, 'space', split_axis=2, concat_axis=1, tiled=T...]
    reshape x15 -> x0, local copies, waits for them, and re-layouts: 38.7 us -> none  [the longest x9 21.6 us: split_heads(): array.reshape(array.shape[0], array.shape[1], array.shape[2] // HEAD_DIM,...]
    all_to_all x15 -> x0, local copies, waits for them, and re-layouts: 32.8 us -> none  [the longest x1 4.8 us: spatial_block(): lax.all_to_all(query_spatial, 'space', split_axis=2, concat_axis=1, tiled...]
    unnamed x26 -> x0, local copies, waits for them, and re-layouts: 24.3 us -> none
    sub x1 -> x0, matrix products: 7.3 us -> none  [attention_core(): attend = jax.nn.softmax(scores, axis=-1)]
  transfers between devices with their start and end apart: 14 -> 0, of which waited for: 9 -> 0; matrix products, arithmetic and copies ran while one was open for 45% -> 0% of each run, Pallas kernels for 0% -> 0%
where the time goes in v1:
time: 358 us
  Pallas kernels  357 us (100%)
    pallas_call x1, Pallas kernels, local(): pl.pallas_call(split, out_shape=[one] * 6, in_specs=[anywhere], out_specs...  216 us
    pallas_call x1, Pallas kernels, local(): pl.pallas_call(core, out_shape=jax.ShapeDtypeStruct((6, frames, rows, wid...  141 us

profile of v1, /device:TPU:1, one launch (start us, length us, event | category | flops | bytes accessed | tf_op | source)
XLA Modules:
  0.0 357.6 jit_solution(10938093210927501855)
XLA Ops:
  0.6 141.4 %core.1.whole = bf16[6,2,96,3072]{3,2,1,0:T(8,128)(2,1)} custom-call(bf16[2,96,3072]{2,1,0:T(8,128)(2,1)} %qs.1, bf16[2,96,3072]{2,1,0:T(8,128)(2,1)} %ks.1, bf16[2,96,3072]{2,1,0:T(8,128)(2,1)} %vs.1, bf16[2,96,3072]{2,1,0:T(8,128)(2,1)} %qt.1, bf16[2,96,3072]{2,1,0:T(8,128)(2,1)} %kt.1, bf16[2,96,3072]{2,1,0:T(8,128)(2,1)} %vt.1, bf16[2,96,3072]{2,1,0:T(8,128)(2,1)} %up.1, ...), custom_call_target="tpu_custom_call" | custom-call | tf_op jit(solution)/shard_map/core/pallas_call | solution.py:205
  142.0 215.6 %split.1 = (bf16[2,96,3072]{2,1,0:T(8,128)(2,1)}, bf16[2,96,3072]{2,1,0:T(8,128)(2,1)}, bf16[2,96,3072]{2,1,0:T(8,128)(2,1)}, bf16[2,96,3072]{2,1,0:T(8,128)(2,1...) custom-call(bf16[6,2,96,3072]{3,2,1,0:T(8,128)(2,1)} %core.1.whole), custom_call_target="tpu_custom_call" | custom-call | tf_op jit(solution)/shard_map/split/pallas_call | solution.py:235

commit v2 on v1

--- a/solution.py
+++ b/solution.py
@@ -1,5 +1,3 @@
-import functools
-
 import jax
 import jax.numpy as jnp
 from jax import lax
@@ -153,10 +151,9 @@
                 remote(g_s.at[:, f, tokens(d), here], out.at[pl.ds(0, 3), f, :, there], gz_sem.at[0], space=d).start()
 
     send_space(0)
-    for i in range(steps):
+    for i in range(2):
         send_time(i)
-        if i == 2:
-            send_space(1)
+    send_space(1)
     pass_time(0)
     for copy in own:
         copy.wait()
@@ -165,6 +162,10 @@
         @pl.when(i + 1 < steps)
         def _():
             pass_time(i + 1)
+
+        @pl.when(i + 2 < steps)
+        def _():
+            send_time(i + 2)
 
         finish_time(i)
         time_step(i)
@@ -187,15 +188,6 @@
         arrived(ref, send_sem.at[0])
 
 
-def split(whole, *rest):
-    outs, sem = rest[:-1], rest[-1]
-    copies = [pltpu.make_async_copy(whole.at[j], o, sem.at[j]) for j, o in enumerate(outs)]
-    for copy in copies:
-        copy.start()
-    for copy in copies:
-        copy.wait()
-
-
 def local(*args):
     up, ws = args[6], args[7]
     frames, rows, width = up.shape
@@ -204,9 +196,9 @@
     anywhere = pl.BlockSpec(memory_space=pl.ANY)
     whole = pl.pallas_call(
         core,
-        out_shape=jax.ShapeDtypeStruct((6, frames, rows, width), bf),
-        in_specs=[anywhere] * 9,
-        out_specs=anywhere,
+        out_shape=pltpu.VMEM((6, frames, rows, width), bf),
+        in_specs=[pl.BlockSpec(memory_space=pltpu.HBM)] * 9,
+        out_specs=pl.BlockSpec(memory_space=pltpu.VMEM),
         scratch_shapes=[
             pltpu.VMEM((frames, 4 * rows, width), bf),
             pltpu.VMEM((4 * frames, rows, width), bf),
@@ -228,18 +220,10 @@
             pltpu.SemaphoreType.DMA((1,)),
         ],
         compiler_params=pltpu.CompilerParams(
-            collective_id=0, has_side_effects=True, vmem_limit_bytes=56 * 1024 * 1024),
+            collective_id=0, has_side_effects=True, vmem_limit_bytes=57 * 1024 * 1024),
         name="core",
     )(*args)
-    one = jax.ShapeDtypeStruct((frames, rows, width), bf)
-    return tuple(pl.pallas_call(
-        split,
-        out_shape=[one] * 6,
-        in_specs=[anywhere],
-        out_specs=[anywhere] * 6,
-        scratch_shapes=[pltpu.SemaphoreType.DMA((6,))],
-        name="split",
-    )(whole))
+    return tuple(whole[j] for j in range(6))
 
 
 def solution(mesh):

time: 358 us -> 131 us (0.37)
  Pallas kernels: 357 us -> 127 us
    pallas_call x2 -> x1, Pallas kernels: 357 us -> 127 us  [local(): pl.pallas_call(core, out_shape=pltpu.VMEM((6, frames, rows, width), bf),...]
where the time goes in v2:
time: 131 us; the launch traced here: 130 us
  Pallas kernels  127 us (97%)
  local copies, waits for them, and re-layouts  3 us (2%)
    pallas_call x1, Pallas kernels, local(): pl.pallas_call(core, out_shape=pltpu.VMEM((6, frames, rows, width), bf),...  127 us
    squeeze x1, local copies, waits for them, and re-layouts, local(): return tuple((whole[j] for j in range(6)))  3 us

profile of v2, /device:TPU:1, one launch (start us, length us, event | category | flops | bytes accessed | tf_op | source)
XLA Modules:
  0.0 130.4 jit_solution(2515996389182379460)
XLA Ops:
  0.6 126.8 %core.1 = bf16[6,2,96,3072]{3,2,1,0:T(8,128)(2,1)S(1)} custom-call(bf16[2,96,3072]{2,1,0:T(8,128)(2,1)} %qs.1, bf16[2,96,3072]{2,1,0:T(8,128)(2,1)} %ks.1, bf16[2,96,3072]{2,1,0:T(8,128)(2,1)} %vs.1, bf16[2,96,3072]{2,1,0:T(8,128)(2,1)} %qt.1, bf16[2,96,3072]{2,1,0:T(8,128)(2,1)} %kt.1, bf16[2,96,3072]{2,1,0:T(8,128)(2,1)} %vt.1, bf16[2,96,3072]{2,1,0:T(8,128)(2,1)} %up.1, ...), custom_call_target="tpu_custom_call" | custom-call | tf_op jit(solution)/shard_map/core/pallas_call | solution.py:197
  127.4 3.0 %slice_bitcast_fusion = (bf16[2,96,3072]{2,1,0:T(8,128)(2,1)}, bf16[2,96,3072]{2,1,0:T(8,128)(2,1)}, bf16[2,96,3072]{2,1,0:T(8,128)(2,1)}, bf16[2,96,3072]{2,1,0...) fusion(bf16[6,2,96,3072]{3,2,1,0:T(8,128)(2,1)S(1)} %core.1), kind=kLoop, calls=%fused_computation | loop fusion | bytes 14155776 | tf_op jit(solution)/shard_map/squeeze | solution.py:226

commit v3 on v2

--- a/solution.py
+++ b/solution.py
@@ -9,7 +9,7 @@
 SCALE = HEAD ** (-0.5)
 MESH = pl.DeviceIdType.MESH
 STEP = 16
-BEFORE_SPATIAL = (2, 4)
+BEFORE_SPATIAL = (1, 3)
 NT = (((1,), (1,)), ((), ()))
 NN = (((1,), (0,)), ((), ()))
 TN = (((0,), (0,)), ((), ()))
@@ -122,9 +122,9 @@
             q, k, v = (a_t[j, :, toks(i), c].reshape(size, HEAD) for j in range(3))
             for j, g in enumerate(attention(q, k, v, og_t[:, c], mask)):
                 g_t[j, :, toks(i), c] = g.reshape(8, STEP, HEAD)
-        pltpu.make_async_copy(g_t.at[:, pl.ds(2 * t, 2), toks(i)], out.at[pl.ds(3, 3), :, toks(i), cols(t)], gy_sem.at[1]).start()
         for d in (y_far, y_up, y_down):
             remote(g_t.at[:, pl.ds(2 * d, 2), toks(i)], out.at[pl.ds(3, 3), :, toks(i), cols(t)], gy_sem.at[0], tm=d).start()
+        pltpu.make_async_copy(g_t.at[:, pl.ds(2 * t, 2), toks(i)], out.at[pl.ds(3, 3), :, toks(i), cols(t)], gy_sem.at[1]).start()
 
     def space_part(f):
         arrived(up_s.at[f, pl.ds(0, rows)], upz_sem.at[f, 0])
@@ -146,13 +146,13 @@
             lax.fori_loop(b * half, (b + 1) * half, head, 0)
             here = pl.ds(b * half * HEAD, half * HEAD)
             there = pl.ds(pl.multiple_of(s * part + b * half * HEAD, HEAD), half * HEAD)
-            pltpu.make_async_copy(g_s.at[:, f, tokens(s), here], out.at[pl.ds(0, 3), f, :, there], gz_sem.at[1]).start()
             for d in (far, cross, pair):
                 remote(g_s.at[:, f, tokens(d), here], out.at[pl.ds(0, 3), f, :, there], gz_sem.at[0], space=d).start()
-
+            pltpu.make_async_copy(g_s.at[:, f, tokens(s), here], out.at[pl.ds(0, 3), f, :, there], gz_sem.at[1]).start()
+
+    send_time(0)
     send_space(0)
-    for i in range(2):
-        send_time(i)
+    send_time(1)
     send_space(1)
     pass_time(0)
     for copy in own:

time: 131 us -> 127 us (0.969)
  Pallas kernels: 127 us -> 123 us
    pallas_call x1, Pallas kernels: 127 us -> 123 us  [local(): pl.pallas_call(core, out_shape=pltpu.VMEM((6, frames, rows, width), bf),...]
where the time goes in v3:
time: 127 us
  Pallas kernels  123 us (97%)
  local copies, waits for them, and re-layouts  3 us (2%)
    pallas_call x1, Pallas kernels, local(): pl.pallas_call(core, out_shape=pltpu.VMEM((6, frames, rows, width), bf),...  123 us
    squeeze x1, local copies, waits for them, and re-layouts, local(): return tuple((whole[j] for j in range(6)))  3 us

profile of v3, /device:TPU:1, one launch (start us, length us, event | category | flops | bytes accessed | tf_op | source)
XLA Modules:
  0.0 126.7 jit_solution(2283268525558872348)
XLA Ops:
  0.6 123.1 %core.1 = bf16[6,2,96,3072]{3,2,1,0:T(8,128)(2,1)S(1)} custom-call(bf16[2,96,3072]{2,1,0:T(8,128)(2,1)} %qs.1, bf16[2,96,3072]{2,1,0:T(8,128)(2,1)} %ks.1, bf16[2,96,3072]{2,1,0:T(8,128)(2,1)} %vs.1, bf16[2,96,3072]{2,1,0:T(8,128)(2,1)} %qt.1, bf16[2,96,3072]{2,1,0:T(8,128)(2,1)} %kt.1, bf16[2,96,3072]{2,1,0:T(8,128)(2,1)} %vt.1, bf16[2,96,3072]{2,1,0:T(8,128)(2,1)} %up.1, ...), custom_call_target="tpu_custom_call" | custom-call | tf_op jit(solution)/shard_map/core/pallas_call | solution.py:197
  123.7 3.0 %slice_bitcast_fusion = (bf16[2,96,3072]{2,1,0:T(8,128)(2,1)}, bf16[2,96,3072]{2,1,0:T(8,128)(2,1)}, bf16[2,96,3072]{2,1,0:T(8,128)(2,1)}, bf16[2,96,3072]{2,1,0...) fusion(bf16[6,2,96,3072]{3,2,1,0:T(8,128)(2,1)S(1)} %core.1), kind=kLoop, calls=%fused_computation | loop fusion | bytes 14155776 | tf_op jit(solution)/shard_map/squeeze | solution.py:226

commit v4 on v3

--- a/solution.py
+++ b/solution.py
@@ -9,7 +9,8 @@
 SCALE = HEAD ** (-0.5)
 MESH = pl.DeviceIdType.MESH
 STEP = 16
-BEFORE_SPATIAL = (1, 3)
+SPATIAL_AFTER = 1
+PIECES = 2
 NT = (((1,), (1,)), ((), ()))
 NN = (((1,), (0,)), ((), ()))
 TN = (((0,), (0,)), ((), ()))
@@ -35,25 +36,33 @@
 
 
 def core(qs, ks, vs, qt, kt, vt, up, ws, wt, out,
-         up_s, up_t, a_s, a_t, w_s, w_t, og_s, og_t, g_s, g_t,
-         own_sem, upz_sem, qkvz_sem, upy_sem, qkvy_sem, gz_sem, gy_sem, send_sem):
+         up_s, up_t, a_s, a_t, w_s, w_t, w_p, og_s, og_t, og_p, g_s, g_t,
+         own_sem, upz_sem, qkvz_sem, upy_sem, qkvy_sem, ogy_sem, wy_sem, wx_sem, wc_sem, gz_sem, gy_sem, send_sem):
     frames, rows, width = up.shape
     part = a_s.shape[-1]
     heads = part // HEAD
     steps = rows // STEP
+    r = lax.axis_index("rep")
     t = lax.axis_index("tm")
     s = lax.axis_index("space")
     n = 4
+    x = r // 2
+    core_id = lax.rem(s, 2)
     y_up, y_down, y_far = lax.rem(t + 1, n), lax.rem(t + n - 1, n), lax.rem(t + 2, n)
-    pair = s + 1 - 2 * lax.rem(s, 2)
+    mate = t + 1 - 2 * lax.rem(t, 2)
+    mirror = n - 1 - t
+    pair = s + 1 - 2 * core_id
     far = lax.rem(s + 2, n)
     cross = lax.rem(pair + 2, n)
+    x_others = [lax.rem(x + k, n) * 2 + lax.rem(r, 2) for k in (1, 3, 2)]
 
     barrier = pltpu.get_barrier_semaphore()
     for d in (y_up, y_down, y_far):
         pl.semaphore_signal(barrier, inc=1, device_id={"tm": d}, device_id_type=MESH)
     for d in (pair, far, cross):
         pl.semaphore_signal(barrier, inc=1, device_id={"space": d}, device_id_type=MESH)
+    for d in x_others:
+        pl.semaphore_signal(barrier, inc=1, device_id={"rep": d}, device_id_type=MESH)
 
     def cols(d):
         return pl.ds(pl.multiple_of(d * part, part), part)
@@ -72,7 +81,7 @@
         pltpu.make_async_copy(ref, ref, sem).wait()
 
     own = [
-        pltpu.make_async_copy(up, up_t.at[pl.ds(2 * t, 2)], own_sem.at[0]),
+        pltpu.make_async_copy(up, up_t.at[pl.ds(0, 2)], own_sem.at[0]),
         pltpu.make_async_copy(wt, w_t, own_sem.at[1]),
         pltpu.make_async_copy(up, up_s.at[:, tokens(s)], own_sem.at[2]),
         pltpu.make_async_copy(ws, w_s, own_sem.at[3]),
@@ -82,7 +91,33 @@
         own.append(pltpu.make_async_copy(src_s.at[:, :, cols(s)], a_s.at[j, :, tokens(s)], own_sem.at[7 + j]))
     for copy in own:
         copy.start()
-    pl.semaphore_wait(barrier, 6)
+    pl.semaphore_wait(barrier, 9)
+
+    block = part // 2 // PIECES
+    quarter = block // n
+
+    def weight_block(p):
+        return pl.ds(pl.multiple_of((2 * p + core_id) * block, block), block)
+
+    def weight_quarter(p):
+        return pl.ds(pl.multiple_of((2 * p + core_id) * block + x * quarter, quarter), quarter)
+
+    def weights_y(p):
+        remote(wt.at[weight_quarter(p)], w_p.at[weight_quarter(p)], wy_sem.at[p], tm=mate).start()
+
+    def weights_x(p):
+        ref = w_p.at[weight_quarter(p)]
+        arrived(ref, wy_sem.at[p])
+        for d in x_others:
+            remote(ref, ref, wx_sem.at[p], rep=d).start()
+
+    def weights_c(p):
+        arrived(w_p.at[pl.ds(0, 3 * quarter)], wx_sem.at[p])
+        ref = w_p.at[weight_block(p)]
+        remote(ref, ref, wc_sem.at[p], space=pair).start()
+
+    def weights_here(p):
+        arrived(w_p.at[pl.ds(0, block)], wc_sem.at[p])
 
     def send_space(f):
         for d, slot in ((far, 0), (pair, 1)):
@@ -91,47 +126,49 @@
             for d in (far, cross, pair):
                 remote(src.at[f, :, cols(d)], a_s.at[j, f, tokens(s)], qkvz_sem.at[f], space=d).start()
 
+    def pass_space(f):
+        arrived(up_s.at[f, pl.ds(0, rows)], upz_sem.at[f, 0])
+        remote(up_s.at[f, tokens(far)], up_s.at[f, tokens(far)], upz_sem.at[f, 2], space=pair).start()
+
+    def finish_space(f):
+        arrived(up_s.at[f, pl.ds(0, rows)], upz_sem.at[f, 1])
+        arrived(up_s.at[f, pl.ds(0, rows)], upz_sem.at[f, 2])
+        arrived(a_s.at[:, f, pl.ds(0, 3 * rows)], qkvz_sem.at[f])
+
     def send_time(i):
-        for d, slot in ((y_up, 0), (y_down, 1)):
-            remote(up.at[:, toks(i)], up_t.at[pl.ds(2 * t, 2), toks(i)], upy_sem.at[i, slot], tm=d).start()
         for j, src in enumerate((qt, kt, vt)):
             for d in (y_up, y_down, y_far):
                 remote(src.at[:, toks(i), cols(d)], a_t.at[j, pl.ds(2 * t, 2), toks(i)], qkvy_sem.at[i], tm=d).start()
 
-    def pass_time(i):
-        arrived(up_t.at[pl.ds(0, 2), toks(i)], upy_sem.at[i, 0])
-        low = 2 * y_down
-        remote(up_t.at[low, toks(i)], up_t.at[low, toks(i)], upy_sem.at[i, 2], tm=y_up).start()
-        arrived(up_t.at[pl.ds(0, 2), toks(i)], upy_sem.at[i, 1])
-        high = 2 * y_up + 1
-        remote(up_t.at[high, toks(i)], up_t.at[high, toks(i)], upy_sem.at[i, 3], tm=y_down).start()
-
-    def finish_time(i):
-        arrived(up_t.at[0, toks(i)], upy_sem.at[i, 2])
-        arrived(up_t.at[0, toks(i)], upy_sem.at[i, 3])
+    def time_arrived(i):
         arrived(a_t.at[:, pl.ds(0, 6), toks(i)], qkvy_sem.at[i])
 
+    def project_own():
+        og = mul(up_t[...].reshape(4 * rows, width), w_t[...], NT).astype(jnp.bfloat16).reshape(4, rows, part)
+        og_t[pl.ds(2 * t, 2)] = og[:2]
+        og_t[pl.ds(2 * mirror, 2)] = og[2:]
+
+    def project_mate():
+        og_p[...] = mul(up_t[...].reshape(4 * rows, width), w_p[...], NT).astype(jnp.bfloat16).reshape(4, rows, part)
+        for i in range(steps):
+            for k, d in ((0, t), (2, mirror)):
+                remote(og_p.at[pl.ds(k, 2), toks(i)], og_t.at[pl.ds(2 * d, 2), toks(i)], ogy_sem.at[i], tm=mate).start()
+
     def time_step(i):
-        x = up_t[:, toks(i), :].reshape(8 * STEP, width)
-        og_t[...] = mul(x, w_t[...], NT).astype(jnp.bfloat16)
         size = 8 * STEP
         mask = (lax.broadcasted_iota(jnp.int32, (size, size), 0) % STEP
                 == lax.broadcasted_iota(jnp.int32, (size, size), 1) % STEP)
         for h in range(heads):
             c = slice(h * HEAD, (h + 1) * HEAD)
             q, k, v = (a_t[j, :, toks(i), c].reshape(size, HEAD) for j in range(3))
-            for j, g in enumerate(attention(q, k, v, og_t[:, c], mask)):
+            o = og_t[:, toks(i), c].reshape(size, HEAD)
+            for j, g in enumerate(attention(q, k, v, o, mask)):
                 g_t[j, :, toks(i), c] = g.reshape(8, STEP, HEAD)
         for d in (y_far, y_up, y_down):
             remote(g_t.at[:, pl.ds(2 * d, 2), toks(i)], out.at[pl.ds(3, 3), :, toks(i), cols(t)], gy_sem.at[0], tm=d).start()
         pltpu.make_async_copy(g_t.at[:, pl.ds(2 * t, 2), toks(i)], out.at[pl.ds(3, 3), :, toks(i), cols(t)], gy_sem.at[1]).start()
 
     def space_part(f):
-        arrived(up_s.at[f, pl.ds(0, rows)], upz_sem.at[f, 0])
-        remote(up_s.at[f, tokens(far)], up_s.at[f, tokens(far)], upz_sem.at[f, 2], space=pair).start()
-        arrived(up_s.at[f, pl.ds(0, rows)], upz_sem.at[f, 1])
-        arrived(up_s.at[f, pl.ds(0, rows)], upz_sem.at[f, 2])
-        arrived(a_s.at[:, f, pl.ds(0, 3 * rows)], qkvz_sem.at[f])
         og_s[...] = mul(up_s[f], w_s[...], NT).astype(jnp.bfloat16)
 
         def head(h, carry):
@@ -150,29 +187,42 @@
                 remote(g_s.at[:, f, tokens(d), here], out.at[pl.ds(0, 3), f, :, there], gz_sem.at[0], space=d).start()
             pltpu.make_async_copy(g_s.at[:, f, tokens(s), here], out.at[pl.ds(0, 3), f, :, there], gz_sem.at[1]).start()
 
+    for p in range(PIECES):
+        weights_y(p)
+    remote(up, up_t.at[pl.ds(2, 2)], upy_sem.at[0], tm=mirror).start()
     send_time(0)
     send_space(0)
     send_time(1)
-    send_space(1)
-    pass_time(0)
     for copy in own:
         copy.wait()
+    for p in range(PIECES):
+        weights_x(p)
+    send_time(2)
+    send_time(3)
+    pass_space(0)
+    send_space(1)
+    for p in range(PIECES):
+        weights_c(p)
+    send_time(4)
+    send_time(5)
+    arrived(up_t.at[pl.ds(2, 2)], upy_sem.at[0])
+    project_own()
+    for p in range(PIECES):
+        weights_here(p)
+    project_mate()
+    finish_space(0)
+    space_part(0)
 
     def step(i, carry):
-        @pl.when(i + 1 < steps)
+        time_arrived(i)
+        arrived(og_t.at[pl.ds(0, 4), toks(i)], ogy_sem.at[i])
+        time_step(i)
+
+        @pl.when(i == SPATIAL_AFTER)
         def _():
-            pass_time(i + 1)
-
-        @pl.when(i + 2 < steps)
-        def _():
-            send_time(i + 2)
-
-        finish_time(i)
-        time_step(i)
-
-        @pl.when((i == BEFORE_SPATIAL[0]) | (i == BEFORE_SPATIAL[1]))
-        def _():
-            space_part(jnp.where(i == BEFORE_SPATIAL[0], 0, 1))
+            pass_space(1)
+            finish_space(1)
+            space_part(1)
         return carry
 
     lax.fori_loop(0, steps, step, 0)
@@ -181,8 +231,10 @@
     arrived(out.at[pl.ds(0, 3), :, :, pl.ds(0, 3 * part)], gz_sem.at[0])
     arrived(out.at[pl.ds(3, 3), :, :, pl.ds(0, part)], gy_sem.at[1])
     arrived(out.at[pl.ds(3, 3), :, :, pl.ds(0, 3 * part)], gy_sem.at[0])
-    for _ in range(6):
+    arrived(w_p, send_sem.at[0])
+    for _ in range(4):
         arrived(up_t.at[pl.ds(0, 2)], send_sem.at[0])
+    arrived(og_p, send_sem.at[0])
     for ref in (a_s.at[:, :, pl.ds(0, 3 * rows)], a_t.at[:, pl.ds(0, 6)]):
         arrived(ref, send_sem.at[0])
         arrived(ref, send_sem.at[0])
@@ -201,20 +253,26 @@
         out_specs=pl.BlockSpec(memory_space=pltpu.VMEM),
         scratch_shapes=[
             pltpu.VMEM((frames, 4 * rows, width), bf),
-            pltpu.VMEM((4 * frames, rows, width), bf),
+            pltpu.VMEM((2 * frames, rows, width), bf),
             pltpu.VMEM((3, frames, 4 * rows, part), bf),
             pltpu.VMEM((3, 4 * frames, rows, part), bf),
             pltpu.VMEM((part, width), bf),
             pltpu.VMEM((part, width), bf),
+            pltpu.VMEM((part, width), bf),
             pltpu.VMEM((4 * rows, part), bf),
-            pltpu.VMEM((4 * frames * STEP, part), bf),
+            pltpu.VMEM((4 * frames, rows, part), bf),
+            pltpu.VMEM((2 * frames, rows, part), bf),
             pltpu.VMEM((3, frames, 4 * rows, part), bf),
             pltpu.VMEM((3, 4 * frames, rows, part), bf),
             pltpu.SemaphoreType.DMA((10,)),
             pltpu.SemaphoreType.DMA((frames, 3)),
             pltpu.SemaphoreType.DMA((frames,)),
-            pltpu.SemaphoreType.DMA((rows // STEP, 4)),
+            pltpu.SemaphoreType.DMA((1,)),
             pltpu.SemaphoreType.DMA((rows // STEP,)),
+            pltpu.SemaphoreType.DMA((rows // STEP,)),
+            pltpu.SemaphoreType.DMA((PIECES,)),
+            pltpu.SemaphoreType.DMA((PIECES,)),
+            pltpu.SemaphoreType.DMA((PIECES,)),
             pltpu.SemaphoreType.DMA((2,)),
             pltpu.SemaphoreType.DMA((2,)),
             pltpu.SemaphoreType.DMA((1,)),

time: 127 us -> 115 us (0.906)
  Pallas kernels: 123 us -> 111 us
    pallas_call x1, Pallas kernels: 123 us -> 111 us  [local(): pl.pallas_call(core, out_shape=pltpu.VMEM((6, frames, rows, width), bf),...]
where the time goes in v4:
time: 115 us
  Pallas kernels  111 us (97%)
  local copies, waits for them, and re-layouts  3 us (3%)
    pallas_call x1, Pallas kernels, local(): pl.pallas_call(core, out_shape=pltpu.VMEM((6, frames, rows, width), bf),...  111 us
    squeeze x1, local copies, waits for them, and re-layouts, local(): return tuple((whole[j] for j in range(6)))  3 us

profile of v4, /device:TPU:1, one launch (start us, length us, event | category | flops | bytes accessed | tf_op | source)
XLA Modules:
  0.0 114.6 jit_solution(303338894287525195)
XLA Ops:
  0.6 110.9 %core.1 = bf16[6,2,96,3072]{3,2,1,0:T(8,128)(2,1)S(1)} custom-call(bf16[2,96,3072]{2,1,0:T(8,128)(2,1)} %qs.1, bf16[2,96,3072]{2,1,0:T(8,128)(2,1)} %ks.1, bf16[2,96,3072]{2,1,0:T(8,128)(2,1)} %vs.1, bf16[2,96,3072]{2,1,0:T(8,128)(2,1)} %qt.1, bf16[2,96,3072]{2,1,0:T(8,128)(2,1)} %kt.1, bf16[2,96,3072]{2,1,0:T(8,128)(2,1)} %vt.1, bf16[2,96,3072]{2,1,0:T(8,128)(2,1)} %up.1, ...), custom_call_target="tpu_custom_call" | custom-call | tf_op jit(solution)/shard_map/core/pallas_call | solution.py:249
  111.6 3.0 %slice_bitcast_fusion = (bf16[2,96,3072]{2,1,0:T(8,128)(2,1)}, bf16[2,96,3072]{2,1,0:T(8,128)(2,1)}, bf16[2,96,3072]{2,1,0:T(8,128)(2,1)}, bf16[2,96,3072]{2,1,0...) fusion(bf16[6,2,96,3072]{3,2,1,0:T(8,128)(2,1)S(1)} %core.1), kind=kLoop, calls=%fused_computation | loop fusion | bytes 14155776 | tf_op jit(solution)/shard_map/squeeze | solution.py:284

commit v5 on v4

--- a/solution.py
+++ b/solution.py
@@ -37,7 +37,7 @@
 
 def core(qs, ks, vs, qt, kt, vt, up, ws, wt, out,
          up_s, up_t, a_s, a_t, w_s, w_t, w_p, og_s, og_t, og_p, g_s, g_t,
-         own_sem, upz_sem, qkvz_sem, upy_sem, qkvy_sem, ogy_sem, wy_sem, wx_sem, wc_sem, gz_sem, gy_sem, send_sem):
+         own_sem, upz_sem, qkvz_sem, upy_sem, qkvy_sem, ogy_sem, wy_sem, wx_sem, wc_sem, gz_sem, gy_sem, send_sem, ready_y, ready_z, ready_x):
     frames, rows, width = up.shape
     part = a_s.shape[-1]
     heads = part // HEAD
@@ -57,12 +57,22 @@
     x_others = [lax.rem(x + k, n) * 2 + lax.rem(r, 2) for k in (1, 3, 2)]
 
     barrier = pltpu.get_barrier_semaphore()
-    for d in (y_up, y_down, y_far):
-        pl.semaphore_signal(barrier, inc=1, device_id={"tm": d}, device_id_type=MESH)
-    for d in (pair, far, cross):
-        pl.semaphore_signal(barrier, inc=1, device_id={"space": d}, device_id_type=MESH)
-    for d in x_others:
-        pl.semaphore_signal(barrier, inc=1, device_id={"rep": d}, device_id_type=MESH)
+    half_z = s // 2
+    y_others = (y_up, y_down, y_far)
+    x_index = [lax.rem(x + k, n) for k in (1, 3, 2)]
+
+    def signal_if(condition, semaphore, **where):
+        @pl.when(condition)
+        def _():
+            pl.semaphore_signal(semaphore, inc=1, device_id=where, device_id_type=MESH)
+
+    pl.semaphore_signal(barrier, inc=1, device_id={"space": pair}, device_id_type=MESH)
+    for d in y_others:
+        signal_if(d > t, barrier, tm=d)
+    for d in (far, cross):
+        signal_if(half_z == 0, barrier, space=d)
+    for k, d in zip(x_index, x_others):
+        signal_if(k > x, barrier, rep=d)
 
     def cols(d):
         return pl.ds(pl.multiple_of(d * part, part), part)
@@ -91,7 +101,13 @@
         own.append(pltpu.make_async_copy(src_s.at[:, :, cols(s)], a_s.at[j, :, tokens(s)], own_sem.at[7 + j]))
     for copy in own:
         copy.start()
-    pl.semaphore_wait(barrier, 9)
+    pl.semaphore_wait(barrier, 1 + t + 2 * half_z + x)
+    for d in y_others:
+        signal_if(d < t, ready_y, tm=d)
+    for d in (far, cross):
+        signal_if(half_z == 1, ready_z, space=d)
+    for k, d in zip(x_index, x_others):
+        signal_if(k < x, ready_x, rep=d)
 
     block = part // 2 // PIECES
     quarter = block // n
@@ -187,12 +203,29 @@
                 remote(g_s.at[:, f, tokens(d), here], out.at[pl.ds(0, 3), f, :, there], gz_sem.at[0], space=d).start()
             pltpu.make_async_copy(g_s.at[:, f, tokens(s), here], out.at[pl.ds(0, 3), f, :, there], gz_sem.at[1]).start()
 
+    @pl.when(half_z == 1)
+    def _():
+        send_space(0)
+
+    @pl.when(t < n - 1)
+    def _():
+        pl.semaphore_wait(ready_y, n - 1 - t)
+
     for p in range(PIECES):
         weights_y(p)
     remote(up, up_t.at[pl.ds(2, 2)], upy_sem.at[0], tm=mirror).start()
     send_time(0)
-    send_space(0)
     send_time(1)
+
+    @pl.when(half_z == 0)
+    def _():
+        pl.semaphore_wait(ready_z, 2)
+        send_space(0)
+
+    @pl.when(x < n - 1)
+    def _():
+        pl.semaphore_wait(ready_x, n - 1 - x)
+
     for copy in own:
         copy.wait()
     for p in range(PIECES):
@@ -276,6 +309,9 @@
             pltpu.SemaphoreType.DMA((2,)),
             pltpu.SemaphoreType.DMA((2,)),
             pltpu.SemaphoreType.DMA((1,)),
+            pltpu.SemaphoreType.REGULAR,
+            pltpu.SemaphoreType.REGULAR,
+            pltpu.SemaphoreType.REGULAR,
         ],
         compiler_params=pltpu.CompilerParams(
             collective_id=0, has_side_effects=True, vmem_limit_bytes=57 * 1024 * 1024),

time: 115 us -> 113 us (0.983)
  Pallas kernels: 111 us -> 109 us
    pallas_call x1, Pallas kernels: 111 us -> 109 us  [local(): pl.pallas_call(core, out_shape=pltpu.VMEM((6, frames, rows, width), bf),...]
where the time goes in v5:
time: 113 us
  Pallas kernels  109 us (96%)
  local copies, waits for them, and re-layouts  3 us (3%)
    pallas_call x1, Pallas kernels, local(): pl.pallas_call(core, out_shape=pltpu.VMEM((6, frames, rows, width), bf),...  109 us
    squeeze x1, local copies, waits for them, and re-layouts, local(): return tuple((whole[j] for j in range(6)))  3 us

profile of v5, /device:TPU:1, one launch (start us, length us, event | category | flops | bytes accessed | tf_op | source)
XLA Modules:
  0.0 112.7 jit_solution(16957523742185147115)
XLA Ops:
  0.6 109.1 %core.1 = bf16[6,2,96,3072]{3,2,1,0:T(8,128)(2,1)S(1)} custom-call(bf16[2,96,3072]{2,1,0:T(8,128)(2,1)} %qs.1, bf16[2,96,3072]{2,1,0:T(8,128)(2,1)} %ks.1, bf16[2,96,3072]{2,1,0:T(8,128)(2,1)} %vs.1, bf16[2,96,3072]{2,1,0:T(8,128)(2,1)} %qt.1, bf16[2,96,3072]{2,1,0:T(8,128)(2,1)} %kt.1, bf16[2,96,3072]{2,1,0:T(8,128)(2,1)} %vt.1, bf16[2,96,3072]{2,1,0:T(8,128)(2,1)} %up.1, ...), custom_call_target="tpu_custom_call" | custom-call | tf_op jit(solution)/shard_map/core/pallas_call | solution.py:282
  109.7 3.0 %slice_bitcast_fusion = (bf16[2,96,3072]{2,1,0:T(8,128)(2,1)}, bf16[2,96,3072]{2,1,0:T(8,128)(2,1)}, bf16[2,96,3072]{2,1,0:T(8,128)(2,1)}, bf16[2,96,3072]{2,1,0...) fusion(bf16[6,2,96,3072]{3,2,1,0:T(8,128)(2,1)S(1)} %core.1), kind=kLoop, calls=%fused_computation | loop fusion | bytes 14155776 | tf_op jit(solution)/shard_map/squeeze | solution.py:320

commit v6 on v5

--- a/solution.py
+++ b/solution.py
@@ -9,7 +9,7 @@
 SCALE = HEAD ** (-0.5)
 MESH = pl.DeviceIdType.MESH
 STEP = 16
-SPATIAL_AFTER = 1
+SPATIAL_AFTER = 2
 PIECES = 2
 NT = (((1,), (1,)), ((), ()))
 NN = (((1,), (0,)), ((), ()))

time: 113 us -> 112 us (level)
    pallas_call x1, Pallas kernels: 109 us -> 108 us  [local(): pl.pallas_call(core, out_shape=pltpu.VMEM((6, frames, rows, width), bf),...]
where the time goes in v6:
time: 112 us
  Pallas kernels  108 us (96%)
  local copies, waits for them, and re-layouts  3 us (3%)
    pallas_call x1, Pallas kernels, local(): pl.pallas_call(core, out_shape=pltpu.VMEM((6, frames, rows, width), bf),...  108 us
    squeeze x1, local copies, waits for them, and re-layouts, local(): return tuple((whole[j] for j in range(6)))  3 us

profile of v6, /device:TPU:1, one launch (start us, length us, event | category | flops | bytes accessed | tf_op | source)
XLA Modules:
  0.0 111.6 jit_solution(7126286866516252891)
XLA Ops:
  0.6 107.9 %core.1 = bf16[6,2,96,3072]{3,2,1,0:T(8,128)(2,1)S(1)} custom-call(bf16[2,96,3072]{2,1,0:T(8,128)(2,1)} %qs.1, bf16[2,96,3072]{2,1,0:T(8,128)(2,1)} %ks.1, bf16[2,96,3072]{2,1,0:T(8,128)(2,1)} %vs.1, bf16[2,96,3072]{2,1,0:T(8,128)(2,1)} %qt.1, bf16[2,96,3072]{2,1,0:T(8,128)(2,1)} %kt.1, bf16[2,96,3072]{2,1,0:T(8,128)(2,1)} %vt.1, bf16[2,96,3072]{2,1,0:T(8,128)(2,1)} %up.1, ...), custom_call_target="tpu_custom_call" | custom-call | tf_op jit(solution)/shard_map/core/pallas_call | solution.py:282
  108.6 3.0 %slice_bitcast_fusion = (bf16[2,96,3072]{2,1,0:T(8,128)(2,1)}, bf16[2,96,3072]{2,1,0:T(8,128)(2,1)}, bf16[2,96,3072]{2,1,0:T(8,128)(2,1)}, bf16[2,96,3072]{2,1,0...) fusion(bf16[6,2,96,3072]{3,2,1,0:T(8,128)(2,1)S(1)} %core.1), kind=kLoop, calls=%fused_computation | loop fusion | bytes 14155776 | tf_op jit(solution)/shard_map/squeeze | solution.py:320

commit v7 on v6

--- a/solution.py
+++ b/solution.py
@@ -99,8 +99,6 @@
     for j, (src_t, src_s) in enumerate(((qt, qs), (kt, ks), (vt, vs))):
         own.append(pltpu.make_async_copy(src_t.at[:, :, cols(t)], a_t.at[j, pl.ds(2 * t, 2)], own_sem.at[4 + j]))
         own.append(pltpu.make_async_copy(src_s.at[:, :, cols(s)], a_s.at[j, :, tokens(s)], own_sem.at[7 + j]))
-    for copy in own:
-        copy.start()
     pl.semaphore_wait(barrier, 1 + t + 2 * half_z + x)
     for d in y_others:
         signal_if(d < t, ready_y, tm=d)
@@ -221,6 +219,9 @@
     def _():
         pl.semaphore_wait(ready_z, 2)
         send_space(0)
+
+    for copy in own:
+        copy.start()
 
     @pl.when(x < n - 1)
     def _():

time: 112 us -> 112 us (level)
  no operation moved by 1% of the time
where the time goes in v7:
time: 112 us
  Pallas kernels  108 us (96%)
  local copies, waits for them, and re-layouts  3 us (3%)
    pallas_call x1, Pallas kernels, local(): pl.pallas_call(core, out_shape=pltpu.VMEM((6, frames, rows, width), bf),...  108 us
    squeeze x1, local copies, waits for them, and re-layouts, local(): return tuple((whole[j] for j in range(6)))  3 us

profile of v7, /device:TPU:1, one launch (start us, length us, event | category | flops | bytes accessed | tf_op | source)
XLA Modules:
  0.0 111.6 jit_solution(16250953126139877723)
XLA Ops:
  0.6 107.9 %core.1 = bf16[6,2,96,3072]{3,2,1,0:T(8,128)(2,1)S(1)} custom-call(bf16[2,96,3072]{2,1,0:T(8,128)(2,1)} %qs.1, bf16[2,96,3072]{2,1,0:T(8,128)(2,1)} %ks.1, bf16[2,96,3072]{2,1,0:T(8,128)(2,1)} %vs.1, bf16[2,96,3072]{2,1,0:T(8,128)(2,1)} %qt.1, bf16[2,96,3072]{2,1,0:T(8,128)(2,1)} %kt.1, bf16[2,96,3072]{2,1,0:T(8,128)(2,1)} %vt.1, bf16[2,96,3072]{2,1,0:T(8,128)(2,1)} %up.1, ...), custom_call_target="tpu_custom_call" | custom-call | tf_op jit(solution)/shard_map/core/pallas_call | solution.py:283
  108.6 3.0 %slice_bitcast_fusion = (bf16[2,96,3072]{2,1,0:T(8,128)(2,1)}, bf16[2,96,3072]{2,1,0:T(8,128)(2,1)}, bf16[2,96,3072]{2,1,0:T(8,128)(2,1)}, bf16[2,96,3072]{2,1,0...) fusion(bf16[6,2,96,3072]{3,2,1,0:T(8,128)(2,1)S(1)} %core.1), kind=kLoop, calls=%fused_computation | loop fusion | bytes 14155776 | tf_op jit(solution)/shard_map/squeeze | solution.py:321
